TPU v7x, 32 devices: a whole 2x2x4 slice. The times are simulated.
32 devices in a mesh: tm: 4 (over x, core), space: 8 (over z, y).
Axes of the slice: x: 2, y: 2, z: 4, core: 2. Of those that a mesh axis runs over, the one named last changes fastest.
Arguments:
- water_depth: float32 [24, 16, 128], P('space'), may hold values from 0.7 to 1.4
- momentum: float32 [24, 2, 16, 128], P('space'), may hold values from -0.6 to 0.6
- slot_live: int32 [24], P('space'), may hold values from 0 to 1, as said below
- neighbours: int32 [24, 2], P('space'), may hold values from 0 to 3, as said below
Outputs:
- slice_ends: float32 [4, 24, 3, 16, 128], P('tm', 'space')
Inputs may be any that keep to these rules, and one draw needn't show every extreme that they name: `slot_live`: every owner's 3 consecutive slots hold between 1 and 3 live blocks; owners 2p and 2p + 1 together hold exactly 4 live blocks, and some owner holds 3. `neighbours`: the live blocks of each owner form one run along the channel, and the runs of owners 0, 1, 2 and so on follow one another around the periodic channel. For a live slot, entry 0 names the slot of the same owner holding the block to the west and entry 1 the one to the east, or 3 where that block belongs to the previous (west) or next (east) owner; each owner has exactly one live slot with entry 0 equal to 3 and one with entry 1 equal to 3. A dead slot names itself in both entries.
All inputs are finite; a program needn't handle non-finite values.
Results may differ from a plain program's by a relative error of at most 0.00002.
Values sent between devices are 32-bit elements; how exact they have to be, the bound alone decides.
No kernel may reach another device: no remote copies, remote signals or barrier semaphores. Data moves between devices by JAX's collectives and lax.ppermute only.
A program may use at most 64 MiB of HBM per device.

v0:
```python
import jax
import jax.numpy as jnp
from jax import lax
from jax.sharding import PartitionSpec as P

SUB = 3
KITER = 2


GRAVITY = 1.0
TIME_STEP = 0.15


def padded_2(x, sides, width):
    for axis, dim in sides:
        size, length = (lax.axis_size(axis), x.shape[dim])
        up = [(i, (i + 1) % size) for i in range(size)]
        down = [(j, i) for i, j in up]
        last = lax.slice_in_dim(x, length - width, length, axis=dim)
        first = lax.slice_in_dim(x, 0, width, axis=dim)
        before = lax.ppermute(last, axis, up)
        after = lax.ppermute(first, axis, down)
        x = jnp.concatenate([before, x, after], axis=dim)
    return x


def shifted(block, axis, distance):
    devices = range(lax.axis_size(axis))
    route = [(i - distance, i) for i in devices if i - distance in devices]
    return lax.ppermute(block, axis, route)


def fluxes(fields, along_ratio, across_ratio):
    height = fields[0]
    drift_along = fields[1] / height
    drift_across = fields[2] / height
    celerity = jnp.sqrt(GRAVITY * height)
    pressure = 0.5 * GRAVITY * height * height
    flux_along = jnp.stack([fields[1], fields[1] * drift_along + pressure, fields[2] * drift_along])
    signal_along = jnp.abs(drift_along) + celerity
    face_along = 0.5 * (flux_along[:, :, :-1] + flux_along[:, :, 1:]) - 0.5 * jnp.maximum(
        signal_along[:, :-1], signal_along[:, 1:]
    ) * (fields[:, :, 1:] - fields[:, :, :-1])
    interior = fields[:, :, 1:-1]
    flux_across = jnp.stack(
        [fields[2], fields[1] * drift_across, fields[2] * drift_across + pressure]
    )[:, :, 1:-1]
    signal_across = (jnp.abs(drift_across) + celerity)[:, 1:-1]
    mirror = jnp.array([1.0, 1.0, -1.0], dtype=jnp.float32)[:, None, None]
    padded = jnp.concatenate(
        [interior[:, :1] * mirror, interior, interior[:, -1:] * mirror], axis=1
    )
    padded_flux = jnp.concatenate(
        [-flux_across[:, :1] * mirror, flux_across, -flux_across[:, -1:] * mirror], axis=1
    )
    padded_signal = jnp.concatenate([signal_across[:1], signal_across, signal_across[-1:]], axis=0)
    face_across = 0.5 * (padded_flux[:, :-1] + padded_flux[:, 1:]) - 0.5 * jnp.maximum(
        padded_signal[:-1], padded_signal[1:]
    ) * (padded[:, 1:] - padded[:, :-1])
    return -along_ratio * (face_along[:, :, 1:] - face_along[:, :, :-1]) - across_ratio * (
        face_across[:, 1:] - face_across[:, :-1]
    )


def heun_step(fields, along_ratio, across_ratio):
    predictor = fields[:, :, 1:-1] + fluxes(fields, along_ratio, across_ratio)
    return 0.5 * (
        fields[:, :, 2:-2] + predictor[:, :, 1:-1] + fluxes(predictor, along_ratio, across_ratio)
    )


def fine_block(fields):
    return heun_step(fields, TIME_STEP, TIME_STEP)


def coarse_block(fields):
    return heun_step(fields, TIME_STEP * SUB, TIME_STEP * SUB / 3.0)


def fine_run(extended):
    fields = extended
    for substep in range(SUB):
        fields = jax.vmap(fine_block)(fields)
    return fields


def restrict(fields):
    return 0.5 * (fields[..., 0::2, :] + fields[..., 1::2, :])


def prolong(fields):
    return jnp.repeat(fields, 2, axis=-2)


def edge_strips(fields, rim_width, first_block, last_block):
    leading = jnp.sum(
        jnp.where(first_block[:, None, None, None], fields[..., :rim_width], 0.0), axis=0
    )
    trailing = jnp.sum(
        jnp.where(last_block[:, None, None, None], fields[..., -rim_width:], 0.0), axis=0
    )
    return jnp.stack([leading.reshape(-1), trailing.reshape(-1)])


def side_strips(fields, rim_width, received, west_slot, east_slot):
    field_count = fields.shape[1]
    row_count = fields.shape[2]
    prior_rim = received[0].reshape(1, field_count, row_count, rim_width)
    next_rim = received[3].reshape(1, field_count, row_count, rim_width)
    west_source = jnp.concatenate([fields[..., -rim_width:], prior_rim], axis=0)
    east_source = jnp.concatenate([fields[..., :rim_width], next_rim], axis=0)
    return (jnp.take(west_source, west_slot, axis=0), jnp.take(east_source, east_slot, axis=0))


def local(water_depth, momentum, slot_live, neighbours):
    blocks = water_depth.shape[0]
    initial = jnp.concatenate([water_depth[:, None], momentum], axis=1)
    slice_index = lax.axis_index("tm")
    first_slice = slice_index == 0
    slice_count = lax.axis_size("tm")
    west_slot = neighbours[:, 0]
    east_slot = neighbours[:, 1]
    live_slot = slot_live == 1
    first_block = jnp.logical_and(west_slot == blocks, live_slot)
    last_block = jnp.logical_and(east_slot == blocks, live_slot)
    rim_width = 2 * SUB

    def coarse_step(current):
        strips = edge_strips(current, 2, first_block, last_block)
        received = padded_2(strips, (("space", 0),), 1)
        west_rim, east_rim = side_strips(current, 2, received, west_slot, east_slot)
        extended = jnp.concatenate([west_rim, current, east_rim], axis=-1)
        return jax.vmap(coarse_block)(extended)

    def run_chain(coarse_start, correction):
        gathered = None
        if correction is not None:
            gathered = lax.all_gather(correction[None], "tm", axis=0, tiled=True)
        current = coarse_start
        own_propagated = coarse_start
        own_state = coarse_start
        for position in range(slice_count):
            own_turn = slice_index == position
            own_state = jnp.where(own_turn, current, own_state)
            propagated = coarse_step(current)
            own_propagated = jnp.where(own_turn, propagated, own_propagated)
            if position + 1 < slice_count:
                current = propagated if gathered is None else propagated + gathered[position]
        return (own_propagated, own_state)

    coarse_start = restrict(initial)
    previous, current = run_chain(coarse_start, None)
    slice_start = jnp.where(first_slice, initial, prolong(current))
    slice_end = slice_start
    for sweep in range(KITER):
        fine_strips = edge_strips(slice_start, rim_width, first_block, last_block)
        fine_received = padded_2(fine_strips, (("space", 0),), 1)
        fine_west_rim, fine_east_rim = side_strips(
            slice_start, rim_width, fine_received, west_slot, east_slot
        )
        refined = fine_run(jnp.concatenate([fine_west_rim, slice_start, fine_east_rim], axis=-1))
        correction = restrict(refined) - previous
        renewed, current = run_chain(coarse_start, correction)
        slice_end = prolong(renewed) + refined - prolong(previous)
        if sweep + 1 < KITER:
            received = shifted(slice_end, "tm", 1)
            slice_start = jnp.where(first_slice, initial, received)
            previous = renewed
    return jnp.where(live_slot[:, None, None, None], slice_end, 0.0)[None]


def solution(mesh):
    placed = (P("space", None, None), P("space", None, None, None), P("space"), P("space", None))
    return jax.shard_map(
        local,
        mesh=mesh,
        in_specs=placed,
        out_specs=P("tm", "space", None, None, None),
        check_vma=False,
    )
```

profile of v0, /device:TPU:0, one launch (start us, length us, event | category | flops | bytes accessed | tf_op | source)
XLA Modules:
  0.0 178.1 jit_solution(13549306103816868852)
XLA Ops:
  0.0 0.8 pad_maximum_fusion.30
  1.8 6.1 %collective-permute-start.1 = (f32[1,48]{1,0:T(1,128)S(1)}, f32[1,48]{1,0:T(1,128)S(1)}, u32[]{:S(2)}, u32[]{:S(2)}) collective-permute-start(f32[1,48]{1,0:T(1,128)S(1)} %stack_reshape.77), channel_id=1, source_target_pairs={{1,0},{2,1},{3,2},{4,3},{5,4},{6,5},{7,6},{0,7},{9,8},{10,9},{11,1... | collective-permute-start | bytes 584 | tf_op jit(solution)/shard_map/ppermute | solution.py:22
  8.1 1.1 collective-permute-done.1
  9.7 0.7 reduce.64
  11.3 2.9 %collective-permute-done = f32[1,48]{1,0:T(1,128)S(1)} collective-permute-done((f32[1,48]{1,0:T(1,128)S(1)}, f32[1,48]{1,0:T(1,128)S(1)}, u32[]{:S(2)}, u32[]{:S(2)}) %collective-permute-start) | collective-permute-done | bytes 224 | tf_op jit(solution)/shard_map/ppermute | solution.py:21
  14.2 0.7 reduce.65
  16.2 0.6 copy-done
  19.0 2.0 %collective-permute-start.3 = (f32[1,48]{1,0:T(1,128)S(1)}, f32[1,48]{1,0:T(1,128)S(1)}, u32[]{:S(2)}, u32[]{:S(2)}) collective-permute-start(f32[1,48]{1,0:T(1,128)S(1)} %stack_reshape.79), channel_id=1, source_target_pairs={{1,0},{2,1},{3,2},{4,3},{5,4},{6,5},{7,6},{0,7},{9,8},{10,9},{11,1... | collective-permute-start | bytes 584 | tf_op jit(solution)/shard_map/ppermute | solution.py:22
  21.3 1.4 collective-permute-done.3
  22.6 0.7 reduce.66
  24.3 3.1 %collective-permute-done.2 = f32[1,48]{1,0:T(1,128)S(1)} collective-permute-done((f32[1,48]{1,0:T(1,128)S(1)}, f32[1,48]{1,0:T(1,128)S(1)}, u32[]{:S(2)}, u32[]{:S(2)}) %collective-permute-start.2) | collective-permute-done | bytes 224 | tf_op jit(solution)/shard_map/ppermute | solution.py:21
  27.5 0.7 reduce.67
  31.6 1.6 collective-permute-start.5
  33.8 1.4 collective-permute-done.5
  35.1 0.7 reduce.68
  36.9 2.7 %collective-permute-done.4 = f32[1,48]{1,0:T(1,128)S(1)} collective-permute-done((f32[1,48]{1,0:T(1,128)S(1)}, f32[1,48]{1,0:T(1,128)S(1)}, u32[]{:S(2)}, u32[]{:S(2)}) %collective-permute-start.4) | collective-permute-done | bytes 224 | tf_op jit(solution)/shard_map/ppermute | solution.py:21
  39.6 0.7 reduce.69
  43.5 0.7 copy-done.1
  44.5 1.6 collective-permute-start.7
  47.0 4.3 %collective-permute-start.9 = (f32[1,48]{1,0:T(1,128)S(1)}, f32[1,48]{1,0:T(1,128)S(1)}, u32[]{:S(2)}, u32[]{:S(2)}) collective-permute-start(f32[1,48]{1,0:T(1,128)S(1)} %stack_reshape.85), channel_id=1, source_target_pairs={{1,0},{2,1},{3,2},{4,3},{5,4},{6,5},{7,6},{0,7},{9,8},{10,9},{11,1... | collective-permute-start | bytes 584 | tf_op jit(solution)/shard_map/ppermute | solution.py:22
  51.6 1.0 collective-permute-done.9
  52.6 0.7 reduce.70
  54.3 3.6 %collective-permute-done.8 = f32[1,48]{1,0:T(1,128)S(1)} collective-permute-done((f32[1,48]{1,0:T(1,128)S(1)}, f32[1,48]{1,0:T(1,128)S(1)}, u32[]{:S(2)}, u32[]{:S(2)}) %collective-permute-start.8) | collective-permute-done | bytes 224 | tf_op jit(solution)/shard_map/ppermute | solution.py:21
  57.8 0.7 reduce.71
  71.8 5.5 %all-gather = f32[12,3,8,128]{3,2,1,0:T(8,128)S(1)} all-gather(f32[3,3,8,128]{3,2,1,0:T(8,128)S(1)} %get-tuple-element.35), channel_id=2, replica_groups=mesh['tm'=4,'space'=8] {'tm'}, dimensions={0}, use_global_device_ids=true | all-gather | bytes 184320 | tf_op jit(solution)/shard_map/all_gather | solution.py:138
  77.5 1.4 collective-permute-start.11
  79.0 0.7 collective-permute-start.10
  79.7 1.4 collective-permute-done.11
  81.1 0.7 reduce.72
  82.8 2.5 %collective-permute-done.10 = f32[1,48]{1,0:T(1,128)S(1)} collective-permute-done((f32[1,48]{1,0:T(1,128)S(1)}, f32[1,48]{1,0:T(1,128)S(1)}, u32[]{:S(2)}, u32[]{:S(2)}) %collective-permute-start.10) | collective-permute-done | bytes 224 | tf_op jit(solution)/shard_map/ppermute | solution.py:21
  85.3 0.7 reduce.73
  89.4 1.6 collective-permute-start.13
  91.6 1.4 collective-permute-done.13
  93.0 0.7 reduce.74
  94.7 2.7 %collective-permute-done.12 = f32[1,48]{1,0:T(1,128)S(1)} collective-permute-done((f32[1,48]{1,0:T(1,128)S(1)}, f32[1,48]{1,0:T(1,128)S(1)}, u32[]{:S(2)}, u32[]{:S(2)}) %collective-permute-start.12) | collective-permute-done | bytes 224 | tf_op jit(solution)/shard_map/ppermute | solution.py:21
  97.4 0.7 reduce.75
  101.5 1.6 collective-permute-start.15
  103.7 1.4 collective-permute-done.15
  105.1 0.7 reduce.76
  106.8 2.7 %collective-permute-done.14 = f32[1,48]{1,0:T(1,128)S(1)} collective-permute-done((f32[1,48]{1,0:T(1,128)S(1)}, f32[1,48]{1,0:T(1,128)S(1)}, u32[]{:S(2)}, u32[]{:S(2)}) %collective-permute-start.14) | collective-permute-done | bytes 224 | tf_op jit(solution)/shard_map/ppermute | solution.py:21
  109.5 0.7 reduce.77
  113.4 1.5 collective-permute-start.16
  115.0 0.9 collective-permute-done.16
  116.1 1.6 collective-permute-start.18
  118.4 1.4 collective-permute-done.18
  120.7 3.4 %collective-permute-done.17 = f32[1,288]{1,0:T(1,128)S(1)} collective-permute-done((f32[1,288]{1,0:T(1,128)S(1)}, f32[1,288]{1,0:T(1,128)S(1)}, u32[]{:S(2)}, u32[]{:S(2)}) %collective-permute-start.17) | collective-permute-done | bytes 1184 | tf_op jit(solution)/shard_map/ppermute | solution.py:21
  133.5 8.4 %all-gather.1 = f32[12,3,8,128]{3,2,1,0:T(8,128)S(1)} all-gather(f32[3,3,8,128]{3,2,1,0:T(8,128)S(1)} %multiply_subtract_fusion), channel_id=3, replica_groups=mesh['tm'=4,'space'=8] {'tm'}, dimensions={0}, use_global_device_ids=true | all-gather | bytes 184320 | tf_op jit(solution)/shard_map/all_gather | solution.py:138
  142.1 0.9 collective-permute-start.20
  143.1 1.3 collective-permute-start.19
  144.3 1.4 collective-permute-done.20
  145.7 0.7 reduce.78
  147.4 2.0 %collective-permute-done.19 = f32[1,48]{1,0:T(1,128)S(1)} collective-permute-done((f32[1,48]{1,0:T(1,128)S(1)}, f32[1,48]{1,0:T(1,128)S(1)}, u32[]{:S(2)}, u32[]{:S(2)}) %collective-permute-start.19) | collective-permute-done | bytes 224 | tf_op jit(solution)/shard_map/ppermute | solution.py:21
  149.4 0.7 reduce.79
  153.4 1.6 collective-permute-start.22
  155.6 1.4 collective-permute-done.22
  157.0 0.7 reduce.80
  158.7 2.7 %collective-permute-done.21 = f32[1,48]{1,0:T(1,128)S(1)} collective-permute-done((f32[1,48]{1,0:T(1,128)S(1)}, f32[1,48]{1,0:T(1,128)S(1)}, u32[]{:S(2)}, u32[]{:S(2)}) %collective-permute-start.21) | collective-permute-done | bytes 224 | tf_op jit(solution)/shard_map/ppermute | solution.py:21
  161.4 0.7 reduce.81
  165.5 1.6 collective-permute-start.24
  167.7 1.4 collective-permute-done.24
  169.1 0.7 reduce.82
  170.8 2.7 %collective-permute-done.23 = f32[1,48]{1,0:T(1,128)S(1)} collective-permute-done((f32[1,48]{1,0:T(1,128)S(1)}, f32[1,48]{1,0:T(1,128)S(1)}, u32[]{:S(2)}, u32[]{:S(2)}) %collective-permute-start.23) | collective-permute-done | bytes 224 | tf_op jit(solution)/shard_map/ppermute | solution.py:21
  173.5 0.7 reduce.83
  177.4 0.7 select_bitcast_fusion
  (846 shorter events, 67.8 us)
Async XLA Ops:
  0.9 0.7 copy-start.3
  0.9 0.7 copy-start.4
  1.8 7.4 %collective-permute-start.1 = (f32[1,48]{1,0:T(1,128)S(1)}, f32[1,48]{1,0:T(1,128)S(1)}, u32[]{:S(2)}, u32[]{:S(2)}) collective-permute-start(f32[1,48]{1,0:T(1,128)S(1)} %stack_reshape.77), channel_id=1, source_target_pairs={{1,0},{2,1},{3,2},{4,3},{5,4},{6,5},{7,6},{0,7},{9,8},{10,9},{11,1... | collective-permute-start | bytes 584 | tf_op jit(solution)/shard_map/ppermute | solution.py:22
  7.9 6.3 %collective-permute-start = (f32[1,48]{1,0:T(1,128)S(1)}, f32[1,48]{1,0:T(1,128)S(1)}, u32[]{:S(2)}, u32[]{:S(2)}) collective-permute-start(f32[1,48]{1,0:T(1,128)S(1)} %stack_reshape.76), channel_id=1, source_target_pairs={{0,1},{1,2},{2,3},{3,4},{4,5},{5,6},{6,7},{7,0},{8,9},{9,10},{10,1... | collective-permute-start | bytes 584 | tf_op jit(solution)/shard_map/ppermute | solution.py:21
  16.2 0.7 copy-start
  19.0 3.6 %collective-permute-start.3 = (f32[1,48]{1,0:T(1,128)S(1)}, f32[1,48]{1,0:T(1,128)S(1)}, u32[]{:S(2)}, u32[]{:S(2)}) collective-permute-start(f32[1,48]{1,0:T(1,128)S(1)} %stack_reshape.79), channel_id=1, source_target_pairs={{1,0},{2,1},{3,2},{4,3},{5,4},{6,5},{7,6},{0,7},{9,8},{10,9},{11,1... | collective-permute-start | bytes 584 | tf_op jit(solution)/shard_map/ppermute | solution.py:22
  21.2 6.3 %collective-permute-start.2 = (f32[1,48]{1,0:T(1,128)S(1)}, f32[1,48]{1,0:T(1,128)S(1)}, u32[]{:S(2)}, u32[]{:S(2)}) collective-permute-start(f32[1,48]{1,0:T(1,128)S(1)} %stack_reshape.78), channel_id=1, source_target_pairs={{0,1},{1,2},{2,3},{3,4},{4,5},{5,6},{6,7},{7,0},{8,9},{9,10},{10,1... | collective-permute-start | bytes 584 | tf_op jit(solution)/shard_map/ppermute | solution.py:21
  31.6 3.6 %collective-permute-start.5 = (f32[1,48]{1,0:T(1,128)S(1)}, f32[1,48]{1,0:T(1,128)S(1)}, u32[]{:S(2)}, u32[]{:S(2)}) collective-permute-start(f32[1,48]{1,0:T(1,128)S(1)} %stack_reshape.81), channel_id=1, source_target_pairs={{1,0},{2,1},{3,2},{4,3},{5,4},{6,5},{7,6},{0,7},{9,8},{10,9},{11,1... | collective-permute-start | bytes 584 | tf_op jit(solution)/shard_map/ppermute | solution.py:22
  33.3 6.3 %collective-permute-start.4 = (f32[1,48]{1,0:T(1,128)S(1)}, f32[1,48]{1,0:T(1,128)S(1)}, u32[]{:S(2)}, u32[]{:S(2)}) collective-permute-start(f32[1,48]{1,0:T(1,128)S(1)} %stack_reshape.80), channel_id=1, source_target_pairs={{0,1},{1,2},{2,3},{3,4},{4,5},{5,6},{6,7},{7,0},{8,9},{9,10},{10,1... | collective-permute-start | bytes 584 | tf_op jit(solution)/shard_map/ppermute | solution.py:21
  43.5 0.8 copy-start.1
  43.5 0.8 copy-start.2
  44.5 15.8 %collective-permute-start.7 = (f32[1,288]{1,0:T(1,128)S(1)}, f32[1,288]{1,0:T(1,128)S(1)}, u32[]{:S(2)}, u32[]{:S(2)}) collective-permute-start(f32[1,288]{1,0:T(1,128)S(1)} %stack_reshape.83), channel_id=1, source_target_pairs={{1,0},{2,1},{3,2},{4,3},{5,4},{6,5},{7,6},{0,7},{9,8},{10,9},{11,1... | collective-permute-start | bytes 3464 | tf_op jit(solution)/shard_map/ppermute | solution.py:22
  46.2 15.2 %collective-permute-start.6 = (f32[1,288]{1,0:T(1,128)S(1)}, f32[1,288]{1,0:T(1,128)S(1)}, u32[]{:S(2)}, u32[]{:S(2)}) collective-permute-start(f32[1,288]{1,0:T(1,128)S(1)} %stack_reshape.82), channel_id=1, source_target_pairs={{0,1},{1,2},{2,3},{3,4},{4,5},{5,6},{6,7},{7,0},{8,9},{9,10},{10,1... | collective-permute-start | bytes 3464 | tf_op jit(solution)/shard_map/ppermute | solution.py:21
  47.0 5.6 %collective-permute-start.9 = (f32[1,48]{1,0:T(1,128)S(1)}, f32[1,48]{1,0:T(1,128)S(1)}, u32[]{:S(2)}, u32[]{:S(2)}) collective-permute-start(f32[1,48]{1,0:T(1,128)S(1)} %stack_reshape.85), channel_id=1, source_target_pairs={{1,0},{2,1},{3,2},{4,3},{5,4},{6,5},{7,6},{0,7},{9,8},{10,9},{11,1... | collective-permute-start | bytes 584 | tf_op jit(solution)/shard_map/ppermute | solution.py:22
  51.4 6.5 %collective-permute-start.8 = (f32[1,48]{1,0:T(1,128)S(1)}, f32[1,48]{1,0:T(1,128)S(1)}, u32[]{:S(2)}, u32[]{:S(2)}) collective-permute-start(f32[1,48]{1,0:T(1,128)S(1)} %stack_reshape.84), channel_id=1, source_target_pairs={{0,1},{1,2},{2,3},{3,4},{4,5},{5,6},{6,7},{7,0},{8,9},{9,10},{10,1... | collective-permute-start | bytes 584 | tf_op jit(solution)/shard_map/ppermute | solution.py:21
  77.5 3.6 %collective-permute-start.11 = (f32[1,48]{1,0:T(1,128)S(1)}, f32[1,48]{1,0:T(1,128)S(1)}, u32[]{:S(2)}, u32[]{:S(2)}) collective-permute-start(f32[1,48]{1,0:T(1,128)S(1)} %stack_reshape.87), channel_id=1, source_target_pairs={{1,0},{2,1},{3,2},{4,3},{5,4},{6,5},{7,6},{0,7},{9,8},{10,9},{11,1... | collective-permute-start | bytes 584 | tf_op jit(solution)/shard_map/ppermute | solution.py:22
  79.0 6.3 %collective-permute-start.10 = (f32[1,48]{1,0:T(1,128)S(1)}, f32[1,48]{1,0:T(1,128)S(1)}, u32[]{:S(2)}, u32[]{:S(2)}) collective-permute-start(f32[1,48]{1,0:T(1,128)S(1)} %stack_reshape.86), channel_id=1, source_target_pairs={{0,1},{1,2},{2,3},{3,4},{4,5},{5,6},{6,7},{7,0},{8,9},{9,10},{10,1... | collective-permute-start | bytes 584 | tf_op jit(solution)/shard_map/ppermute | solution.py:21
  89.4 3.6 %collective-permute-start.13 = (f32[1,48]{1,0:T(1,128)S(1)}, f32[1,48]{1,0:T(1,128)S(1)}, u32[]{:S(2)}, u32[]{:S(2)}) collective-permute-start(f32[1,48]{1,0:T(1,128)S(1)} %stack_reshape.89), channel_id=1, source_target_pairs={{1,0},{2,1},{3,2},{4,3},{5,4},{6,5},{7,6},{0,7},{9,8},{10,9},{11,1... | collective-permute-start | bytes 584 | tf_op jit(solution)/shard_map/ppermute | solution.py:22
  91.1 6.3 %collective-permute-start.12 = (f32[1,48]{1,0:T(1,128)S(1)}, f32[1,48]{1,0:T(1,128)S(1)}, u32[]{:S(2)}, u32[]{:S(2)}) collective-permute-start(f32[1,48]{1,0:T(1,128)S(1)} %stack_reshape.88), channel_id=1, source_target_pairs={{0,1},{1,2},{2,3},{3,4},{4,5},{5,6},{6,7},{7,0},{8,9},{9,10},{10,1... | collective-permute-start | bytes 584 | tf_op jit(solution)/shard_map/ppermute | solution.py:21
  101.5 3.6 %collective-permute-start.15 = (f32[1,48]{1,0:T(1,128)S(1)}, f32[1,48]{1,0:T(1,128)S(1)}, u32[]{:S(2)}, u32[]{:S(2)}) collective-permute-start(f32[1,48]{1,0:T(1,128)S(1)} %stack_reshape.91), channel_id=1, source_target_pairs={{1,0},{2,1},{3,2},{4,3},{5,4},{6,5},{7,6},{0,7},{9,8},{10,9},{11,1... | collective-permute-start | bytes 584 | tf_op jit(solution)/shard_map/ppermute | solution.py:22
  103.2 6.3 %collective-permute-start.14 = (f32[1,48]{1,0:T(1,128)S(1)}, f32[1,48]{1,0:T(1,128)S(1)}, u32[]{:S(2)}, u32[]{:S(2)}) collective-permute-start(f32[1,48]{1,0:T(1,128)S(1)} %stack_reshape.90), channel_id=1, source_target_pairs={{0,1},{1,2},{2,3},{3,4},{4,5},{5,6},{6,7},{7,0},{8,9},{9,10},{10,1... | collective-permute-start | bytes 584 | tf_op jit(solution)/shard_map/ppermute | solution.py:21
  113.4 2.4 %collective-permute-start.16 = (f32[3,3,16,128]{3,2,1,0:T(8,128)S(1)}, f32[3,3,16,128]{3,2,1,0:T(8,128)S(1)}, u32[]{:S(2)}, u32[]{:S(2)}) collective-permute-start(f32[3,3,16,128]{3,2,1,0:T(8,128)S(1)} %add_subtract_fusion), channel_id=1, source_target_pairs={{0,8},{8,16},{16,24},{1,9},{9,17},{17,25},{2,10},{10,18},{18,26},{... | collective-permute-start | bytes 221192 | tf_op jit(solution)/shard_map/ppermute | solution.py:30
  116.1 3.6 %collective-permute-start.18 = (f32[1,288]{1,0:T(1,128)S(1)}, f32[1,288]{1,0:T(1,128)S(1)}, u32[]{:S(2)}, u32[]{:S(2)}) collective-permute-start(f32[1,288]{1,0:T(1,128)S(1)} %stack_reshape.93), channel_id=1, source_target_pairs={{1,0},{2,1},{3,2},{4,3},{5,4},{6,5},{7,6},{0,7},{9,8},{10,9},{11,1... | collective-permute-start | bytes 3464 | tf_op jit(solution)/shard_map/ppermute | solution.py:22
  117.8 6.3 %collective-permute-start.17 = (f32[1,288]{1,0:T(1,128)S(1)}, f32[1,288]{1,0:T(1,128)S(1)}, u32[]{:S(2)}, u32[]{:S(2)}) collective-permute-start(f32[1,288]{1,0:T(1,128)S(1)} %stack_reshape.92), channel_id=1, source_target_pairs={{0,1},{1,2},{2,3},{3,4},{4,5},{5,6},{6,7},{7,0},{8,9},{9,10},{10,1... | collective-permute-start | bytes 3464 | tf_op jit(solution)/shard_map/ppermute | solution.py:21
  142.1 3.6 %collective-permute-start.20 = (f32[1,48]{1,0:T(1,128)S(1)}, f32[1,48]{1,0:T(1,128)S(1)}, u32[]{:S(2)}, u32[]{:S(2)}) collective-permute-start(f32[1,48]{1,0:T(1,128)S(1)} %stack_reshape.95), channel_id=1, source_target_pairs={{1,0},{2,1},{3,2},{4,3},{5,4},{6,5},{7,6},{0,7},{9,8},{10,9},{11,1... | collective-permute-start | bytes 584 | tf_op jit(solution)/shard_map/ppermute | solution.py:22
  143.1 6.3 %collective-permute-start.19 = (f32[1,48]{1,0:T(1,128)S(1)}, f32[1,48]{1,0:T(1,128)S(1)}, u32[]{:S(2)}, u32[]{:S(2)}) collective-permute-start(f32[1,48]{1,0:T(1,128)S(1)} %stack_reshape.94), channel_id=1, source_target_pairs={{0,1},{1,2},{2,3},{3,4},{4,5},{5,6},{6,7},{7,0},{8,9},{9,10},{10,1... | collective-permute-start | bytes 584 | tf_op jit(solution)/shard_map/ppermute | solution.py:21
  153.4 3.6 %collective-permute-start.22 = (f32[1,48]{1,0:T(1,128)S(1)}, f32[1,48]{1,0:T(1,128)S(1)}, u32[]{:S(2)}, u32[]{:S(2)}) collective-permute-start(f32[1,48]{1,0:T(1,128)S(1)} %stack_reshape.97), channel_id=1, source_target_pairs={{1,0},{2,1},{3,2},{4,3},{5,4},{6,5},{7,6},{0,7},{9,8},{10,9},{11,1... | collective-permute-start | bytes 584 | tf_op jit(solution)/shard_map/ppermute | solution.py:22
  155.1 6.3 %collective-permute-start.21 = (f32[1,48]{1,0:T(1,128)S(1)}, f32[1,48]{1,0:T(1,128)S(1)}, u32[]{:S(2)}, u32[]{:S(2)}) collective-permute-start(f32[1,48]{1,0:T(1,128)S(1)} %stack_reshape.96), channel_id=1, source_target_pairs={{0,1},{1,2},{2,3},{3,4},{4,5},{5,6},{6,7},{7,0},{8,9},{9,10},{10,1... | collective-permute-start | bytes 584 | tf_op jit(solution)/shard_map/ppermute | solution.py:21
  165.5 3.6 %collective-permute-start.24 = (f32[1,48]{1,0:T(1,128)S(1)}, f32[1,48]{1,0:T(1,128)S(1)}, u32[]{:S(2)}, u32[]{:S(2)}) collective-permute-start(f32[1,48]{1,0:T(1,128)S(1)} %stack_reshape.99), channel_id=1, source_target_pairs={{1,0},{2,1},{3,2},{4,3},{5,4},{6,5},{7,6},{0,7},{9,8},{10,9},{11,1... | collective-permute-start | bytes 584 | tf_op jit(solution)/shard_map/ppermute | solution.py:22
  167.2 6.3 %collective-permute-start.23 = (f32[1,48]{1,0:T(1,128)S(1)}, f32[1,48]{1,0:T(1,128)S(1)}, u32[]{:S(2)}, u32[]{:S(2)}) collective-permute-start(f32[1,48]{1,0:T(1,128)S(1)} %stack_reshape.98), channel_id=1, source_target_pairs={{0,1},{1,2},{2,3},{3,4},{4,5},{5,6},{6,7},{7,0},{8,9},{9,10},{10,1... | collective-permute-start | bytes 584 | tf_op jit(solution)/shard_map/ppermute | solution.py:21
where the time goes:
time: 179 us; the launch traced here: 178 us
  waiting for transfers between devices  46.3 us (26%)
  other arithmetic  40.6 us (23%)
  local copies, waits for them, and re-layouts  39.4 us (22%)
  starting transfers between devices  33.5 us (19%)
  blocking collectives  13.9 us (8%)
  between operations  4.44 us (2%)
    ppermute x12, waiting for transfers between devices, padded_2(): before = lax.ppermute(last, axis, up)  31.1 us
    ppermute x12, starting transfers between devices, padded_2(): after = lax.ppermute(first, axis, down)  26 us
    ppermute x12, waiting for transfers between devices, padded_2(): after = lax.ppermute(first, axis, down)  14.4 us
    all_gather x2, blocking collectives, run_chain(): gathered = lax.all_gather(correction[None], 'tm', axis=0, tiled=True)  13.9 us
    gather x24, local copies, waits for them, and re-layouts, side_strips(): jnp.take(east_source, east_slot, axis=0)  8.45 us
    gather x24, local copies, waits for them, and re-layouts, side_strips(): jnp.take(west_source, west_slot, axis=0)  8.45 us
    ppermute x12, other arithmetic, padded_2(): after = lax.ppermute(first, axis, down)  6.68 us
    ppermute x12, other arithmetic, padded_2(): before = lax.ppermute(last, axis, up)  6.68 us
  transfers between devices with their start and end apart: 25, of which 23 were waited for; matrix products, arithmetic and copies ran while one was open for 13% of the time, Pallas kernels for 0%

commit v1 on v0

v1 whole, which is shorter than its diff:
```python
import functools

import jax
import jax.numpy as jnp
from jax import lax
from jax.experimental import pallas as pl
from jax.experimental.pallas import tpu as pltpu
from jax.sharding import PartitionSpec as P

SUB = 3
KITER = 2
TIME_STEP = 0.15


def lane_of(shape):
    return lax.broadcasted_iota(jnp.int32, shape, 1)


def row_of(shape):
    return lax.broadcasted_iota(jnp.int32, shape, 0)


class Scheme:
    def __init__(self, shape, linked):
        self.rows, self.lanes = shape
        self.linked = linked
        lane, row = lane_of(shape), row_of(shape)
        self.is_first_lane = lane == 0
        self.is_last_lane = lane == self.lanes - 1
        self.is_first_row = row == 0
        self.is_last_row = row == self.rows - 1

    def east(self, tiles):
        rolled = [pltpu.roll(tile, self.lanes - 1, 1) for tile in tiles]
        if not self.linked:
            return rolled
        return [
            jnp.where(self.is_last_lane, rolled[k + 1], rolled[k]) if k + 1 < len(rolled) else rolled[k]
            for k in range(len(rolled))
        ]

    def west(self, tiles):
        rolled = [pltpu.roll(tile, 1, 1) for tile in tiles]
        if not self.linked:
            return rolled
        return [jnp.where(self.is_first_lane, rolled[k - 1], rolled[k]) if k else rolled[k] for k in range(len(rolled))]

    def above(self, tile):
        return pltpu.roll(tile, self.rows - 1, 0)

    def below(self, tile):
        return pltpu.roll(tile, 1, 0)

    def derived(self, state):
        out = []
        for h, hu, hv in zip(*state):
            root = lax.rsqrt(h)
            celerity = h * root
            inverse = root * root
            u = hu * inverse
            q = hv * inverse
            p = (0.5 * h) * h
            out.append(
                (h, hu, hv, hu * u + p, hv * u, hv * q + p, jnp.abs(u) + celerity, jnp.abs(q) + celerity)
            )
        return out

    def along(self, parts):
        h, hu, hv, f1, f2, _, speed, _ = ([part[i] for part in parts] for i in range(8))
        speed_e = self.east(speed)
        values_e = [self.east(h), self.east(hu), self.east(hv)]
        fluxes_e = [values_e[1], self.east(f1), self.east(f2)]
        bound = [jnp.maximum(a, b) for a, b in zip(speed, speed_e)]
        differences = []
        for value, flux, value_e, flux_e in zip((h, hu, hv), (hu, f1, f2), values_e, fluxes_e):
            face = [
                (f + fe) - m * (ve - v) for f, fe, m, v, ve in zip(flux, flux_e, bound, value, value_e)
            ]
            differences.append([e - w for e, w in zip(face, self.west(face))])
        return differences

    @staticmethod
    def cross(lower, upper):
        bound = jnp.maximum(lower[7], upper[7])
        return [
            (lower[f] + upper[f]) - bound * (upper[v] - lower[v]) for v, f in ((0, 2), (1, 4), (2, 5))
        ]

    def upper_faces(self, top, raised):
        faces = self.cross(top, raised)
        wall = 2.0 * (top[5] + top[7] * top[2])
        return [
            jnp.where(self.is_last_row, 0.0, faces[0]),
            jnp.where(self.is_last_row, 0.0, faces[1]),
            jnp.where(self.is_last_row, wall, faces[2]),
        ]

    def lower_faces(self, bottom, faces):
        wall = 2.0 * (bottom[5] - bottom[7] * bottom[2])
        lowered = [self.below(face) for face in faces]
        return [lowered[0], lowered[1], jnp.where(self.is_first_row, wall, lowered[2])]

    def raise_up(self, part):
        return [self.above(part[i]) if i in (0, 1, 2, 4, 5, 7) else None for i in range(8)]

    def fine_rhs(self, even, odd):
        even_parts, odd_parts = self.derived(even), self.derived(odd)
        even_x, odd_x = self.along(even_parts), self.along(odd_parts)
        even_out, odd_out = [[], [], []], [[], [], []]
        scale = -0.5 * TIME_STEP
        for k, (a, b) in enumerate(zip(even_parts, odd_parts)):
            inner = self.cross(a, b)
            upper = self.upper_faces(b, self.raise_up(a))
            lower = self.lower_faces(a, upper)
            for i in range(3):
                even_out[i].append(scale * (even_x[i][k] + (inner[i] - lower[i])))
                odd_out[i].append(scale * (odd_x[i][k] + (upper[i] - inner[i])))
        return even_out, odd_out

    def coarse_rhs(self, state):
        parts = self.derived(state)
        x = self.along(parts)
        out = [[], [], []]
        scale_x, scale_y = -0.5 * TIME_STEP * SUB, -0.5 * TIME_STEP * SUB / 3.0
        for k, a in enumerate(parts):
            upper = self.upper_faces(a, self.raise_up(a))
            lower = self.lower_faces(a, upper)
            for i in range(3):
                out[i].append(scale_x * x[i][k] + scale_y * (upper[i] - lower[i]))
        return out

    @staticmethod
    def plus(a, b):
        return [[s + t for s, t in zip(u, v)] for u, v in zip(a, b)]

    @staticmethod
    def minus(a, b):
        return [[s - t for s, t in zip(u, v)] for u, v in zip(a, b)]

    @staticmethod
    def half(a):
        return [[0.5 * s for s in u] for u in a]

    def coarse(self, state):
        first = self.plus(state, self.coarse_rhs(state))
        return self.half(self.plus(self.plus(state, first), self.coarse_rhs(first)))

    def fine(self, pair):
        for _ in range(SUB):
            first = [self.plus(s, r) for s, r in zip(pair, self.fine_rhs(*pair))]
            pair = [
                self.half(self.plus(self.plus(s, f), r)) for s, f, r in zip(pair, first, self.fine_rhs(*first))
            ]
        return pair

    def restrict(self, pair):
        return self.half(self.plus(pair[0], pair[1]))


class Parareal:
    def __init__(self, scheme, initial):
        self.scheme = scheme
        self.initial = initial
        self.known = {}

    def memo(self, key, build):
        if key not in self.known:
            self.known[key] = build()
        return self.known[key]

    def coarse_state(self, sweep, n):
        sweep = min(sweep, n)

        def build():
            s = self.scheme
            if n == 0:
                return s.restrict(self.initial)
            stepped = self.coarse_step(sweep, n - 1)
            if sweep == 0:
                return stepped
            correction = s.minus(s.restrict(self.fine_run(sweep, n - 1)), self.coarse_step(sweep - 1, n - 1))
            return s.plus(stepped, correction)

        return self.memo(("c", sweep, n), build)

    def coarse_step(self, sweep, n):
        sweep = min(sweep, n)
        return self.memo(("k", sweep, n), lambda: self.scheme.coarse(self.coarse_state(sweep, n)))

    def fine_run(self, sweep, n):
        sweep = 1 if n == 0 else sweep

        def build():
            if n == 0:
                start = self.initial
            elif sweep == 1:
                state = self.coarse_state(0, n)
                start = [state, state]
            else:
                start = self.end(sweep - 1, n - 1)
            return self.scheme.fine(start)

        return self.memo(("f", sweep, n), build)

    def end(self, sweep, n):
        def build():
            s = self.scheme
            refined = self.fine_run(sweep, n)
            renewed, previous = self.coarse_step(sweep, n), self.coarse_step(sweep - 1, n)
            return [s.minus(s.plus(renewed, part), previous) for part in refined]

        return self.memo(("e", sweep, n), build)


def run_of(live_ref, near_ref, blocks):
    first = jnp.int32(0)
    last = jnp.int32(0)
    for slot in range(blocks):
        first = jnp.where((live_ref[slot] == 1) & (near_ref[slot, 0] == blocks), slot, first)
        last = jnp.where((live_ref[slot] == 1) & (near_ref[slot, 1] == blocks), slot, last)
    return first, last


def load_pair(depth_ref, momentum_ref, slot):
    rows = depth_ref.shape[1] // 2
    return [
        [
            depth_ref[slot, pl.ds(parity, rows, stride=2), :],
            momentum_ref[slot, 0, pl.ds(parity, rows, stride=2), :],
            momentum_ref[slot, 1, pl.ds(parity, rows, stride=2), :],
        ]
        for parity in range(2)
    ]


def pack(pieces, start, rim):
    rows, lanes = pieces[0].shape
    lane = lane_of((rows, lanes))
    per_tile = lanes // rim
    tiles = []
    for i, piece in enumerate(pieces):
        place = (i % per_tile) * rim
        moved = pltpu.roll(piece, (place - start) % lanes, 1)
        if place == 0:
            tiles.append(moved)
        else:
            tiles[-1] = jnp.where(lane >= place, moved, tiles[-1])
    return tiles


def unpack(packed_ref, index, place, rim):
    rows, lanes = packed_ref.shape[1:]
    per_tile = lanes // rim
    source = (index % per_tile) * rim
    return pltpu.roll(packed_ref[index // per_tile], (place - source) % lanes, 1)


def send_east_kernel(rim, depth_ref, momentum_ref, live_ref, near_ref, out_ref):
    blocks, _, lanes = depth_ref.shape
    _, last = run_of(live_ref, near_ref, blocks)
    even, odd = load_pair(depth_ref, momentum_ref, last)
    for i, tile in enumerate(pack([*even, *odd], lanes - rim, rim)):
        out_ref[i] = tile


def interior_kernel(
    rim, slices, depth_ref, momentum_ref, live_ref, near_ref, out_ref, send_ref, edge_ref
):
    blocks, height, lanes = depth_ref.shape
    rows = height // 2
    first, last = run_of(live_ref, near_ref, blocks)
    slots = [first]
    for _ in range(blocks - 1):
        following = near_ref[slots[-1], 1]
        slots.append(jnp.where(following < blocks, following, slots[-1]))
    count = sum(live_ref[slot] for slot in range(blocks))

    first_even, first_odd = load_pair(depth_ref, momentum_ref, first)
    last_even, last_odd = load_pair(depth_ref, momentum_ref, last)
    for i, tile in enumerate(pack([*first_even, *first_odd], 0, rim)):
        send_ref[i] = tile
    lane = lane_of((rows, lanes))
    for i, (head, tail) in enumerate(zip([*first_even, *first_odd], [*last_even, *last_odd])):
        if edge_ref.shape[0] == 1:
            edge_ref[0, i] = jnp.where(lane < 2 * rim, head, pltpu.roll(tail, 4 * rim, 1))
        else:
            edge_ref[0, i] = head
            edge_ref[1, i] = pltpu.roll(tail, lanes // 2, 1)

    out_ref[...] = jnp.zeros(out_ref.shape, out_ref.dtype)
    loaded = [load_pair(depth_ref, momentum_ref, slot) for slot in slots]
    initial = [[[pair[parity][i] for pair in loaded] for i in range(3)] for parity in range(2)]
    own = lax.axis_index("tm")
    for n in range(slices):

        @pl.when(own == n)
        def _(n=n):
            ending = Parareal(Scheme((rows, lanes), True), initial).end(KITER, n)
            for k, slot in enumerate(slots):

                @pl.when(k < count)
                def _(k=k, slot=slot):
                    for parity in range(2):
                        for i in range(3):
                            out_ref[slot, i, pl.ds(parity, rows, stride=2), :] = ending[parity][i][k]


def edge_kernel(rim, slices, inner_ref, edge_ref, west_ref, east_ref, live_ref, near_ref, out_ref):
    blocks, _, height, lanes = inner_ref.shape
    rows = height // 2
    tiles = edge_ref.shape[0]
    lane = lane_of((rows, lanes))
    first, last = run_of(live_ref, near_ref, blocks)
    pieces = []
    for i in range(6):
        west = unpack(west_ref, i, lanes - rim, rim)
        if tiles == 1:
            east = unpack(east_ref, i, 4 * rim, rim)
            own = jnp.where(lane < 4 * rim, edge_ref[0, i], east)
            pieces.append([jnp.where(lane < lanes - rim, own, west)])
        else:
            east = unpack(east_ref, i, lanes // 2, rim)
            pieces.append(
                [
                    jnp.where(lane < lanes - rim, edge_ref[0, i], west),
                    jnp.where(lane < lanes // 2, edge_ref[1, i], east),
                ]
            )
    initial = [pieces[:3], pieces[3:]]
    out_ref[...] = inner_ref[...]
    own = lax.axis_index("tm")
    for n in range(slices):

        @pl.when(own == n)
        def _(n=n):
            ending = Parareal(Scheme((rows, lanes), False), initial).end(KITER, n)
            turn = -4 * rim if tiles == 1 else lanes // 2
            for parity in range(2):
                for i in range(3):
                    rows_at = pl.ds(parity, rows, stride=2)
                    result = ending[parity][i]
                    out_ref[first, i, rows_at, :] = jnp.where(lane < rim, result[0], out_ref[first, i, rows_at, :])
                    tail = pltpu.roll(result[-1], turn % lanes, 1)
                    out_ref[last, i, rows_at, :] = jnp.where(
                        lane >= lanes - rim, tail, out_ref[last, i, rows_at, :]
                    )


def local(water_depth, momentum, slot_live, neighbours):
    blocks, height, lanes = water_depth.shape
    rows = height // 2
    slices = lax.axis_size("tm")
    owners = lax.axis_size("space")
    rim = 2 * (slices - 1) + 2 * SUB * KITER - 2
    strip = jax.ShapeDtypeStruct((-(-6 // (lanes // rim)), rows, lanes), jnp.float32)
    edge = jax.ShapeDtypeStruct((1 if 6 * rim <= lanes else 2, 6, rows, lanes), jnp.float32)
    whole = jax.ShapeDtypeStruct((blocks, 3, height, lanes), jnp.float32)
    vmem = pl.BlockSpec(memory_space=pltpu.VMEM)
    smem = pl.BlockSpec(memory_space=pltpu.SMEM)
    up = [(i, (i + 1) % owners) for i in range(owners)]
    down = [(j, i) for i, j in up]

    params = pltpu.CompilerParams(vmem_limit_bytes=16 * 1024 * 1024)
    east_rim = pl.pallas_call(
        functools.partial(send_east_kernel, rim),
        out_shape=strip,
        in_specs=[vmem, vmem, smem, smem],
        out_specs=vmem,
        compiler_params=params,
        name="send_east",
    )(water_depth, momentum, slot_live, neighbours)
    from_west = lax.ppermute(east_rim, "space", up)
    inner, west_rim, edges = pl.pallas_call(
        functools.partial(interior_kernel, rim, slices),
        out_shape=(whole, strip, edge),
        in_specs=[vmem, vmem, smem, smem],
        out_specs=(vmem, vmem, vmem),
        compiler_params=params,
        cost_estimate=pl.CostEstimate(flops=20_000_000, bytes_accessed=200_000, transcendentals=0),
        name="interior",
    )(water_depth, momentum, slot_live, neighbours)
    from_east = lax.ppermute(west_rim, "space", down)
    ends = pl.pallas_call(
        functools.partial(edge_kernel, rim, slices),
        out_shape=whole,
        in_specs=[vmem, vmem, vmem, vmem, smem, smem],
        out_specs=vmem,
        compiler_params=params,
        name="edges",
    )(inner, edges, from_west, from_east, slot_live, neighbours)
    return ends[None]


def solution(mesh):
    placed = (P("space", None, None), P("space", None, None, None), P("space"), P("space", None))
    return jax.shard_map(
        local,
        mesh=mesh,
        in_specs=placed,
        out_specs=P("tm", "space", None, None, None),
        check_vma=False,
    )
```

time: 179 us -> 17.3 us (0.10)
  the two profiles are of different devices: /device:TPU:0 before, /device:TPU:31 now
where the time goes in v1:
time: 17.3 us; the launch traced here: 17.1 us
  Pallas kernels  9.53 us (55%)
  waiting for transfers between devices  3.7 us (21%)
  local copies, waits for them, and re-layouts  2.32 us (13%)
  starting transfers between devices  1.51 us (9%)
    pallas_call x1, Pallas kernels, local(): pl.pallas_call(functools.partial(interior_kernel, rim, slices), out_shape...  4.89 us
    pallas_call x1, Pallas kernels, local(): pl.pallas_call(functools.partial(edge_kernel, rim, slices), out_shape=who...  4 us
    ppermute x1, waiting for transfers between devices, local(): from_east = lax.ppermute(west_rim, 'space', down)  3.7 us
    unnamed x7, local copies, waits for them, and re-layouts  2.32 us
    ppermute x1, starting transfers between devices, local(): from_east = lax.ppermute(west_rim, 'space', down)  1.51 us
    pallas_call x1, Pallas kernels, local(): pl.pallas_call(functools.partial(send_east_kernel, rim), out_shape=strip,...  0.64 us
  transfers between devices with their start and end apart: 2, of which 1 were waited for; matrix products, arithmetic and copies ran while one was open for 0% of the time, Pallas kernels for 29%

profile of v1, /device:TPU:31, one launch (start us, length us, event | category | flops | bytes accessed | tf_op | source)
XLA Modules:
  0.0 17.1 jit_solution(5372785718853450467)
XLA Ops:
  0.0 0.0 copy-start.2
  0.0 0.8 %copy.5.near_ref = s32[3,2]{1,0:T(4,128)S(1)} copy(s32[3,2]{0,1:T(2,128)} %param.7) | data formatting | bytes 48 | tf_op args[3]
  0.8 0.0 copy-done.2
  0.8 0.0 copy-start
  0.8 0.8 %copy-done = f32[3,2,16,128]{3,2,1,0:T(8,128)S(1)} copy-done((f32[3,2,16,128]{3,2,1,0:T(8,128)S(1)}, f32[3,2,16,128]{3,2,1,0:T(8,128)}, u32[]{:S(2)}) %copy-start) | copy-done | bytes 49176
  1.6 0.0 copy-start.1
  1.6 0.7 %copy-done.1 = f32[3,16,128]{2,1,0:T(8,128)S(1)} copy-done((f32[3,16,128]{2,1,0:T(8,128)S(1)}, f32[3,16,128]{2,1,0:T(8,128)}, u32[]{:S(2)}) %copy-start.1) | copy-done | bytes 24600
  2.3 0.6 %send_east.1 = f32[1,8,128]{2,1,0:T(8,128)S(1)} custom-call(f32[3,16,128]{2,1,0:T(8,128)S(1)} %copy-done.1, f32[3,2,16,128]{3,2,1,0:T(8,128)S(1)} %copy-done, s32[3]{0:T(128)S(1)} %copy-done.2, s32[3,2]{1,0:T(4,128)S(1)} %copy.5.near_ref), custom_call_target="tpu_custom_call" | custom-call | tf_op jit(solution)/shard_map/send_east/pallas_call | solution.py:364
  3.0 0.0 collective-permute-start
  3.0 4.9 %interior.1 = (f32[3,3,16,128]{3,2,1,0:T(8,128)S(1)}, f32[1,8,128]{2,1,0:T(8,128)S(1)}, f32[1,6,8,128]{3,2,1,0:T(8,128)S(1)}) custom-call(f32[3,16,128]{2,1,0:T(8,128)S(1)} %copy-done.1, f32[3,2,16,128]{3,2,1,0:T(8,128)S(1)} %copy-done, s32[3]{0:T(128)S(1)} %copy-done.2, s32[3,2]{1,0:T(4,128)S(1)} %copy.5.near_ref), custom_call_target="tpu_custom_call" | custom-call | flops 20000000 | bytes 200000 | tf_op jit(solution)/shard_map/interior/pallas_call | solution.py:373
  7.9 1.5 %collective-permute-start.1 = (f32[1,8,128]{2,1,0:T(8,128)S(1)}, f32[1,8,128]{2,1,0:T(8,128)S(1)}, u32[]{:S(2)}, u32[]{:S(2)}) collective-permute-start(f32[1,8,128]{2,1,0:T(8,128)S(1)} %get-tuple-element.10), channel_id=1, source_target_pairs={{1,0},{2,1},{3,2},{4,3},{5,4},{6,5},{7,6},{0,7},{9,8},{10,9},{11,1... | collective-permute-start | bytes 12296 | tf_op jit(solution)/shard_map/ppermute | solution.py:382
  9.4 0.0 collective-permute-done.west_ref
  9.4 3.7 %collective-permute-done.1.east_ref = f32[1,8,128]{2,1,0:T(8,128)S(1)} collective-permute-done((f32[1,8,128]{2,1,0:T(8,128)S(1)}, f32[1,8,128]{2,1,0:T(8,128)S(1)}, u32[]{:S(2)}, u32[]{:S(2)}) %collective-permute-start.1) | collective-permute-done | bytes 4128 | tf_op jit(solution)/shard_map/ppermute | solution.py:382
  13.1 4.0 %edges.1 = f32[3,3,16,128]{3,2,1,0:T(8,128)} custom-call(f32[3,3,16,128]{3,2,1,0:T(8,128)S(1)} %get-tuple-element.8.inner_ref, f32[1,6,8,128]{3,2,1,0:T(8,128)S(1)} %get-tuple-element.9.edge_ref, f32[1,8,128]{2,1,0:T(8,128)S(1)} %collective-permute-done.west_ref, f32[1,8,128]{2,1,0:T(8,128)S(1)} %collective-permute-done.1.east_ref, s32[3]{0:T(128)S(1)} %copy-done.2, ...), custom_call_target="tpu_custom_call" | custom-call | tf_op jit(solution)/shard_map/edges/pallas_call | solution.py:383
Async XLA Ops:
  0.0 0.8 %copy-start.2 = (s32[3]{0:T(128)S(1)}, s32[3]{0:T(128)}, u32[]{:S(2)}) copy-start(s32[3]{0:T(128)} %live_ref.5) | copy-start | bytes 40
  0.8 0.8 %copy-start = (f32[3,2,16,128]{3,2,1,0:T(8,128)S(1)}, f32[3,2,16,128]{3,2,1,0:T(8,128)}, u32[]{:S(2)}) copy-start(f32[3,2,16,128]{3,2,1,0:T(8,128)} %momentum_ref.3) | copy-start | bytes 147460
  1.6 0.7 %copy-start.1 = (f32[3,16,128]{2,1,0:T(8,128)S(1)}, f32[3,16,128]{2,1,0:T(8,128)}, u32[]{:S(2)}) copy-start(f32[3,16,128]{2,1,0:T(8,128)} %depth_ref.3) | copy-start | bytes 73732
  3.0 6.4 %collective-permute-start = (f32[1,8,128]{2,1,0:T(8,128)S(1)}, f32[1,8,128]{2,1,0:T(8,128)S(1)}, u32[]{:S(2)}, u32[]{:S(2)}) collective-permute-start(f32[1,8,128]{2,1,0:T(8,128)S(1)} %send_east.1), channel_id=1, source_target_pairs={{0,1},{1,2},{2,3},{3,4},{4,5},{5,6},{6,7},{7,0},{8,9},{9,10},{10,1... | collective-permute-start | bytes 12296 | tf_op jit(solution)/shard_map/ppermute | solution.py:372
  7.9 5.2 %collective-permute-start.1 = (f32[1,8,128]{2,1,0:T(8,128)S(1)}, f32[1,8,128]{2,1,0:T(8,128)S(1)}, u32[]{:S(2)}, u32[]{:S(2)}) collective-permute-start(f32[1,8,128]{2,1,0:T(8,128)S(1)} %get-tuple-element.10), channel_id=1, source_target_pairs={{1,0},{2,1},{3,2},{4,3},{5,4},{6,5},{7,6},{0,7},{9,8},{10,9},{11,1... | collective-permute-start | bytes 12296 | tf_op jit(solution)/shard_map/ppermute | solution.py:382

commit v2 on v1

v2 whole, which is shorter than its diff:
```python
import functools

import jax
import jax.numpy as jnp
from jax import lax
from jax.experimental import pallas as pl
from jax.experimental.pallas import tpu as pltpu
from jax.sharding import PartitionSpec as P

SUB = 3
KITER = 2
TIME_STEP = 0.15


def lane_of(shape):
    return lax.broadcasted_iota(jnp.int32, shape, 1)


def row_of(shape):
    return lax.broadcasted_iota(jnp.int32, shape, 0)


class Scheme:
    def __init__(self, shape, linked, mode):
        self.rows, self.lanes = shape
        self.linked = linked
        self.mode = mode
        lane, row = lane_of(shape), row_of(shape)
        self.is_first_lane = lane == 0
        self.is_last_lane = lane == self.lanes - 1
        self.is_first_row = row == 0
        self.is_last_row = row == self.rows - 1

    def east(self, tiles):
        rolled = [pltpu.roll(tile, self.lanes - 1, 1) for tile in tiles]
        if not self.linked:
            return rolled
        return [
            jnp.where(self.is_last_lane, rolled[k + 1], rolled[k]) if k + 1 < len(rolled) else rolled[k]
            for k in range(len(rolled))
        ]

    def west(self, tiles):
        rolled = [pltpu.roll(tile, 1, 1) for tile in tiles]
        if not self.linked:
            return rolled
        return [jnp.where(self.is_first_lane, rolled[k - 1], rolled[k]) if k else rolled[k] for k in range(len(rolled))]

    def above(self, tile):
        return pltpu.roll(tile, self.rows - 1, 0)

    def below(self, tile):
        return pltpu.roll(tile, 1, 0)

    @staticmethod
    def derive(h, hu, hv, needed=(3, 4, 5, 6, 7)):
        root = lax.rsqrt(h)
        celerity = h * root
        inverse = root * root
        u = hu * inverse
        p = (0.5 * h) * h
        part = [h, hu, hv, hu * u + p, hv * u, None, jnp.abs(u) + celerity, None]
        if 5 in needed:
            q = hv * inverse
            part[5] = hv * q + p
            part[7] = jnp.abs(q) + celerity
        return part

    def derived(self, state):
        return [self.derive(h, hu, hv) for h, hu, hv in zip(*state)]

    def moved(self, parts, shift):
        if self.mode == "fields":
            states = zip(*(shift([part[i] for part in parts]) for i in (0, 1, 2)))
            return [self.derive(h, hu, hv, ()) for h, hu, hv in states]
        columns = {i: shift([part[i] for part in parts]) for i in (0, 1, 2, 3, 4, 6)}
        return [[columns[i][k] if i in columns else None for i in range(8)] for k in range(len(parts))]

    @staticmethod
    def faces_along(lower, upper):
        bound = jnp.maximum(lower[6], upper[6])
        return [(lower[f] + upper[f]) - bound * (upper[v] - lower[v]) for v, f in ((0, 1), (1, 3), (2, 4))]

    def along(self, parts):
        east = [self.faces_along(a, b) for a, b in zip(parts, self.moved(parts, self.east))]
        if self.mode == "serial":
            west = list(zip(*(self.west([face[i] for face in east]) for i in range(3))))
        else:
            west = [self.faces_along(a, b) for a, b in zip(self.moved(parts, self.west), parts)]
        return [[e[i] - w[i] for e, w in zip(east, west)] for i in range(3)]

    @staticmethod
    def cross(lower, upper):
        bound = jnp.maximum(lower[7], upper[7])
        return [
            (lower[f] + upper[f]) - bound * (upper[v] - lower[v]) for v, f in ((0, 2), (1, 4), (2, 5))
        ]

    def upper_faces(self, top, raised):
        faces = self.cross(top, raised)
        wall = 2.0 * (top[5] + top[7] * top[2])
        return [
            jnp.where(self.is_last_row, 0.0, faces[0]),
            jnp.where(self.is_last_row, 0.0, faces[1]),
            jnp.where(self.is_last_row, wall, faces[2]),
        ]

    def lower_faces(self, bottom, faces):
        wall = 2.0 * (bottom[5] - bottom[7] * bottom[2])
        lowered = [self.below(face) for face in faces]
        return [lowered[0], lowered[1], jnp.where(self.is_first_row, wall, lowered[2])]

    def raise_up(self, part):
        return [self.above(part[i]) if i in (0, 1, 2, 4, 5, 7) else None for i in range(8)]

    def fine_change(self, even, odd):
        even_parts, odd_parts = self.derived(even), self.derived(odd)
        even_x, odd_x = self.along(even_parts), self.along(odd_parts)
        even_out, odd_out = [[], [], []], [[], [], []]
        for k, (a, b) in enumerate(zip(even_parts, odd_parts)):
            inner = self.cross(a, b)
            upper = self.upper_faces(b, self.raise_up(a))
            lower = self.lower_faces(a, upper)
            for i in range(3):
                even_out[i].append(even_x[i][k] + (inner[i] - lower[i]))
                odd_out[i].append(odd_x[i][k] + (upper[i] - inner[i]))
        return even_out, odd_out

    def coarse_change(self, state):
        parts = self.derived(state)
        x = self.along(parts)
        out = [[], [], []]
        for k, a in enumerate(parts):
            upper = self.upper_faces(a, self.raise_up(a))
            lower = self.lower_faces(a, upper)
            for i in range(3):
                out[i].append(SUB * x[i][k] + (upper[i] - lower[i]))
        return out

    @staticmethod
    def plus(a, b):
        return [[s + t for s, t in zip(u, v)] for u, v in zip(a, b)]

    @staticmethod
    def minus(a, b):
        return [[s - t for s, t in zip(u, v)] for u, v in zip(a, b)]

    @staticmethod
    def times(a, factor):
        return [[factor * s for s in u] for u in a]

    def heun(self, states, change):
        start = change(*states)
        first = [self.minus(s, self.times(c, 0.5 * TIME_STEP)) for s, c in zip(states, start)]
        following = change(*first)
        return [
            self.minus(s, self.times(self.plus(c, d), 0.25 * TIME_STEP)) for s, c, d in zip(states, start, following)
        ]

    def coarse(self, state):
        return self.heun([state], lambda one: [self.coarse_change(one)])[0]

    def fine(self, pair):
        for _ in range(SUB):
            pair = self.heun(pair, self.fine_change)
        return pair

    def restrict(self, pair):
        return self.times(self.plus(pair[0], pair[1]), 0.5)


class Parareal:
    def __init__(self, scheme, initial):
        self.scheme = scheme
        self.initial = initial
        self.known = {}

    def memo(self, key, build):
        if key not in self.known:
            self.known[key] = build()
        return self.known[key]

    def coarse_state(self, sweep, n):
        sweep = min(sweep, n)

        def build():
            s = self.scheme
            if n == 0:
                return s.restrict(self.initial)
            stepped = self.coarse_step(sweep, n - 1)
            if sweep == 0:
                return stepped
            correction = s.minus(s.restrict(self.fine_run(sweep, n - 1)), self.coarse_step(sweep - 1, n - 1))
            return s.plus(stepped, correction)

        return self.memo(("c", sweep, n), build)

    def coarse_step(self, sweep, n):
        sweep = min(sweep, n)
        return self.memo(("k", sweep, n), lambda: self.scheme.coarse(self.coarse_state(sweep, n)))

    def fine_run(self, sweep, n):
        sweep = 1 if n == 0 else sweep

        def build():
            if n == 0:
                start = self.initial
            elif sweep == 1:
                state = self.coarse_state(0, n)
                start = [state, state]
            else:
                start = self.end(sweep - 1, n - 1)
            return self.scheme.fine(start)

        return self.memo(("f", sweep, n), build)

    def end(self, sweep, n):
        def build():
            s = self.scheme
            refined = self.fine_run(sweep, n)
            renewed, previous = self.coarse_step(sweep, n), self.coarse_step(sweep - 1, n)
            return [s.minus(s.plus(renewed, part), previous) for part in refined]

        return self.memo(("e", sweep, n), build)


def run_of(live_ref, near_ref, blocks):
    slot = jnp.int32(0)
    count = jnp.int32(0)
    for k in range(blocks):
        slot = jnp.where((live_ref[k] == 1) & (near_ref[0, k] == blocks), k, slot)
        count += live_ref[k]
    slots = [slot]
    for _ in range(blocks - 1):
        following = near_ref[1, slots[-1]]
        slots.append(jnp.where(following < blocks, following, slots[-1]))
    return slots, count


def load_fields(depth_ref, momentum_ref, slot):
    rows = depth_ref.shape[1] // 2
    return [
        ref[pl.ds(parity, rows, stride=2), :]
        for parity in range(2)
        for ref in (depth_ref.at[slot], momentum_ref.at[slot, 0], momentum_ref.at[slot, 1])
    ]


def pack(pieces, start, rim):
    rows, lanes = pieces[0].shape
    lane = lane_of((rows, lanes))
    per_tile = lanes // rim
    tiles = []
    for i, piece in enumerate(pieces):
        place = (i % per_tile) * rim
        moved = pltpu.roll(piece, (place - start) % lanes, 1)
        if place == 0:
            tiles.append(moved)
        else:
            tiles[-1] = jnp.where(lane >= place, moved, tiles[-1])
    return tiles


def unpack(packed_ref, index, place, rim):
    lanes = packed_ref.shape[2]
    per_tile = lanes // rim
    source = (index % per_tile) * rim
    return pltpu.roll(packed_ref[index // per_tile], (place - source) % lanes, 1)


def send_kernel(
    rim, depth_hbm, momentum_hbm, live_hbm, near_hbm, east_ref, west_ref, run_ref, edge_ref, place_ref,
    depth_ref, momentum_ref, live_ref, near_ref, sems,
):
    copies = [
        pltpu.make_async_copy(source, target, sems.at[i])
        for i, (source, target) in enumerate(
            ((live_hbm, live_ref), (near_hbm, near_ref), (depth_hbm, depth_ref), (momentum_hbm, momentum_ref))
        )
    ]
    for copy in copies:
        copy.start()
    for copy in copies:
        copy.wait()
    blocks, height, lanes = depth_ref.shape
    rows = height // 2
    slots, count = run_of(live_ref, near_ref, blocks)
    tiles = [load_fields(depth_ref, momentum_ref, slot) for slot in slots]
    first, last = tiles[0], tiles[-1]
    for i, tile in enumerate(pack(last, lanes - rim, rim)):
        east_ref[i] = tile
    for i, tile in enumerate(pack(first, 0, rim)):
        west_ref[i] = tile
    for k, fields in enumerate(tiles):
        for i in range(6):
            run_ref[k, i] = fields[i]
        place_ref[k] = jnp.full((rows, lanes), jnp.where(k < count, slots[k], -1), jnp.int32)
    lane = lane_of((rows, lanes))
    for i, (head, tail) in enumerate(zip(first, last)):
        if edge_ref.shape[0] == 1:
            edge_ref[0, i] = jnp.where(lane < 2 * rim, head, pltpu.roll(tail, 4 * rim, 1))
        else:
            edge_ref[0, i] = head
            edge_ref[1, i] = pltpu.roll(tail, lanes // 2, 1)


def as_initial(tiles):
    return [[[tile[3 * parity + i] for tile in tiles] for i in range(3)] for parity in range(2)]


def interior_kernel(slices, run_ref, out_ref):
    blocks, _, rows, lanes = run_ref.shape
    own = lax.axis_index("tm")
    for n in range(slices):

        @pl.when(own == n)
        def _(n=n):
            tiles = [[run_ref[k, i] for i in range(6)] for k in range(blocks)]
            ending = Parareal(Scheme((rows, lanes), True, "serial"), as_initial(tiles)).end(KITER, n)
            for k in range(blocks):
                for i in range(6):
                    out_ref[k, i] = ending[i // 3][i % 3][k]


def edge_kernel(rim, slices, inner_ref, edge_ref, west_ref, east_ref, place_ref, out_ref):
    blocks, _, rows, lanes = inner_ref.shape
    edges = edge_ref.shape[0]
    own = lax.axis_index("tm")
    for n in range(slices):

        @pl.when(own == n)
        def _(n=n):
            lane = lane_of((rows, lanes))
            tiles = [[] for _ in range(edges)]
            for i in range(6):
                west = unpack(west_ref, i, lanes - rim, rim)
                east_start = 4 * rim if edges == 1 else lanes // 2
                east = unpack(east_ref, i, east_start, rim)
                tiles[-1].append(jnp.where(lane < east_start, edge_ref[edges - 1, i], east))
                tiles[0][i:] = [jnp.where(lane < lanes - rim, tiles[0][i] if edges == 1 else edge_ref[0, i], west)]
            ending = Parareal(Scheme((rows, lanes), False, "both"), as_initial(tiles)).end(KITER, n)
            places = [place_ref[k] for k in range(blocks)]
            lasts = [
                (places[k] >= 0) & (places[k + 1] < 0) if k + 1 < blocks else places[k] >= 0 for k in range(blocks)
            ]
            for i in range(6):
                result = ending[i // 3][i % 3]
                tail = pltpu.roll(result[-1], (-4 * rim if edges == 1 else lanes // 2) % lanes, 1)
                merged = []
                for k in range(blocks):
                    tile = jnp.where(lasts[k] & (lane >= lanes - rim), tail, inner_ref[k, i])
                    merged.append(jnp.where(lane < rim, result[0], tile) if k == 0 else tile)
                for slot in range(blocks):
                    chosen = jnp.zeros((rows, lanes), jnp.float32)
                    for k in range(blocks):
                        chosen = jnp.where(places[k] == slot, merged[k], chosen)
                    out_ref[slot, i % 3, pl.ds(i // 3, rows, stride=2), :] = chosen


def local(water_depth, momentum, slot_live, neighbours):
    blocks, height, lanes = water_depth.shape
    rows = height // 2
    slices = lax.axis_size("tm")
    owners = lax.axis_size("space")
    rim = 2 * (slices - 1) + 2 * SUB * KITER - 2
    strip = jax.ShapeDtypeStruct((-(-6 // (lanes // rim)), rows, lanes), jnp.float32)
    edge = jax.ShapeDtypeStruct((1 if 6 * rim <= lanes else 2, 6, rows, lanes), jnp.float32)
    run = jax.ShapeDtypeStruct((blocks, 6, rows, lanes), jnp.float32)
    place = jax.ShapeDtypeStruct((blocks, rows, lanes), jnp.int32)
    whole = jax.ShapeDtypeStruct((blocks, 3, height, lanes), jnp.float32)
    vmem = pl.BlockSpec(memory_space=pltpu.VMEM)
    hbm = pl.BlockSpec(memory_space=pltpu.HBM)
    up = [(i, (i + 1) % owners) for i in range(owners)]
    down = [(j, i) for i, j in up]

    params = pltpu.CompilerParams(vmem_limit_bytes=16 * 1024 * 1024)
    east_rim, west_rim, tiles, edges, places = pl.pallas_call(
        functools.partial(send_kernel, rim),
        out_shape=(strip, strip, run, edge, place),
        in_specs=[hbm] * 4,
        out_specs=(vmem,) * 5,
        scratch_shapes=[
            pltpu.VMEM(water_depth.shape, jnp.float32),
            pltpu.VMEM(momentum.shape, jnp.float32),
            pltpu.SMEM(slot_live.shape, jnp.int32),
            pltpu.SMEM(neighbours.shape[::-1], jnp.int32),
            pltpu.SemaphoreType.DMA((4,)),
        ],
        compiler_params=params,
        name="send",
    )(*(pltpu.with_memory_space_constraint(x, pltpu.HBM) for x in (water_depth, momentum, slot_live, neighbours.T)))
    from_west = lax.ppermute(east_rim, "space", up)
    from_east = lax.ppermute(west_rim, "space", down)
    inner = pl.pallas_call(
        functools.partial(interior_kernel, slices),
        out_shape=run,
        in_specs=[vmem],
        out_specs=vmem,
        compiler_params=params,
        cost_estimate=pl.CostEstimate(flops=20_000_000, bytes_accessed=200_000, transcendentals=0),
        name="interior",
    )(tiles)
    ends = pl.pallas_call(
        functools.partial(edge_kernel, rim, slices),
        out_shape=whole,
        in_specs=[vmem] * 5,
        out_specs=vmem,
        compiler_params=params,
        name="edges",
    )(inner, edges, from_west, from_east, places)
    return ends[None]


def solution(mesh):
    placed = (P("space", None, None), P("space", None, None, None), P("space"), P("space", None))
    return jax.shard_map(
        local,
        mesh=mesh,
        in_specs=placed,
        out_specs=P("tm", "space", None, None, None),
        check_vma=False,
    )
```

time: 17.3 us -> 12.3 us (0.71)
  the two profiles are of different devices: /device:TPU:31 before, /device:TPU:3 now
where the time goes in v2:
time: 12.3 us; the launch traced here: 12.1 us
  Pallas kernels  7.66 us (62%)
  starting transfers between devices  4.4 us (36%)
    pallas_call x1, Pallas kernels, local(): pl.pallas_call(functools.partial(interior_kernel, slices), out_shape=run,...  3.88 us
    ppermute x1, starting transfers between devices, local(): from_east = lax.ppermute(west_rim, 'space', down)  3.1 us
    pallas_call x1, Pallas kernels, local(): pl.pallas_call(functools.partial(edge_kernel, rim, slices), out_shape=who...  2.84 us
    ppermute x1, starting transfers between devices, local(): from_west = lax.ppermute(east_rim, 'space', up)  1.29 us
    pallas_call x1, Pallas kernels, local(): pl.pallas_call(functools.partial(send_kernel, rim), out_shape=(strip, str...  0.95 us
  transfers between devices with their start and end apart: 2, of which 0 were waited for; matrix products, arithmetic and copies ran while one was open for 0% of the time, Pallas kernels for 32%

profile of v2, /device:TPU:3, one launch (start us, length us, event | category | flops | bytes accessed | tf_op | source)
XLA Modules:
  0.0 12.1 jit_solution(10620847522206250788)
XLA Ops:
  0.0 0.9 %send.1 = (f32[1,8,128]{2,1,0:T(8,128)S(1)}, f32[1,8,128]{2,1,0:T(8,128)S(1)}, f32[3,6,8,128]{3,2,1,0:T(8,128)S(1)}, f32[1,6,8,128]{3,2,1,0:T(8,128)S(1)}, s32[3,8,128]{2,1,0:T(8,128)S(1)}) custom-call(f32[3,16,128]{2,1,0:T(8,128)} %depth_hbm.1, f32[3,2,16,128]{3,2,1,0:T(8,128)} %momentum_hbm.1, s32[3]{0:T(128)} %live_hbm.1, s32[2,3]{1,0:T(2,128)} %bitcast.2), custom_call_target="tpu_custom_call" | custom-call | tf_op jit(solution)/shard_map/send/pallas_call | solution.py:377
  1.0 1.3 %collective-permute-start = (f32[1,8,128]{2,1,0:T(8,128)S(1)}, f32[1,8,128]{2,1,0:T(8,128)S(1)}, u32[]{:S(2)}, u32[]{:S(2)}) collective-permute-start(f32[1,8,128]{2,1,0:T(8,128)S(1)} %get-tuple-element.12), channel_id=1, source_target_pairs={{0,1},{1,2},{2,3},{3,4},{4,5},{5,6},{6,7},{7,0},{8,9},{9,10},{10,1... | collective-permute-start | bytes 12296 | tf_op jit(solution)/shard_map/ppermute | solution.py:392
  2.2 3.1 %collective-permute-start.1 = (f32[1,8,128]{2,1,0:T(8,128)S(1)}, f32[1,8,128]{2,1,0:T(8,128)S(1)}, u32[]{:S(2)}, u32[]{:S(2)}) collective-permute-start(f32[1,8,128]{2,1,0:T(8,128)S(1)} %get-tuple-element.13), channel_id=1, source_target_pairs={{1,0},{2,1},{3,2},{4,3},{5,4},{6,5},{7,6},{0,7},{9,8},{10,9},{11,1... | collective-permute-start | bytes 12296 | tf_op jit(solution)/shard_map/ppermute | solution.py:393
  5.4 3.9 %interior.1.inner_ref = f32[3,6,8,128]{3,2,1,0:T(8,128)S(1)} custom-call(f32[3,6,8,128]{3,2,1,0:T(8,128)S(1)} %get-tuple-element.10.run_ref), custom_call_target="tpu_custom_call" | custom-call | flops 20000000 | bytes 200000 | tf_op jit(solution)/shard_map/interior/pallas_call | solution.py:394
  9.2 0.0 collective-permute-done.west_ref
  9.2 0.0 collective-permute-done.1.east_ref
  9.3 2.8 %edges.1 = f32[3,3,16,128]{3,2,1,0:T(8,128)} custom-call(f32[3,6,8,128]{3,2,1,0:T(8,128)S(1)} %interior.1.inner_ref, f32[1,6,8,128]{3,2,1,0:T(8,128)S(1)} %get-tuple-element.11.edge_ref, f32[1,8,128]{2,1,0:T(8,128)S(1)} %collective-permute-done.west_ref, f32[1,8,128]{2,1,0:T(8,128)S(1)} %collective-permute-done.1.east_ref, ...), custom_call_target="tpu_custom_call" | custom-call | tf_op jit(solution)/shard_map/edges/pallas_call | solution.py:403
Async XLA Ops:
  1.0 8.3 %collective-permute-start = (f32[1,8,128]{2,1,0:T(8,128)S(1)}, f32[1,8,128]{2,1,0:T(8,128)S(1)}, u32[]{:S(2)}, u32[]{:S(2)}) collective-permute-start(f32[1,8,128]{2,1,0:T(8,128)S(1)} %get-tuple-element.12), channel_id=1, source_target_pairs={{0,1},{1,2},{2,3},{3,4},{4,5},{5,6},{6,7},{7,0},{8,9},{9,10},{10,1... | collective-permute-start | bytes 12296 | tf_op jit(solution)/shard_map/ppermute | solution.py:392
  2.2 7.0 %collective-permute-start.1 = (f32[1,8,128]{2,1,0:T(8,128)S(1)}, f32[1,8,128]{2,1,0:T(8,128)S(1)}, u32[]{:S(2)}, u32[]{:S(2)}) collective-permute-start(f32[1,8,128]{2,1,0:T(8,128)S(1)} %get-tuple-element.13), channel_id=1, source_target_pairs={{1,0},{2,1},{3,2},{4,3},{5,4},{6,5},{7,6},{0,7},{9,8},{10,9},{11,1... | collective-permute-start | bytes 12296 | tf_op jit(solution)/shard_map/ppermute | solution.py:393
